TPU v7x, 128 devices: a whole 4x4x4 slice. The times are simulated.
128 devices in a mesh: group: 16 (over y, z), tensor: 8 (over x, core).
Axes of the slice: x: 4, y: 4, z: 4, core: 2. Of those that a mesh axis runs over, the one named last changes fastest.
Arguments:
- query: bfloat16 [4096, 8192], P('group', 'tensor'), may hold values from -4.5 to 4.5
- resp_key: bfloat16 [4096, 1024], P('group', 'tensor'), may hold values from -4.5 to 4.5
- resp_value: bfloat16 [4096, 1024], P('group', 'tensor'), may hold values from -4.5 to 4.5
- prefix_key: bfloat16 [4096, 1024], P('group', 'tensor'), may hold values from -4.5 to 4.5
- prefix_value: bfloat16 [4096, 1024], P('group', 'tensor'), may hold values from -4.5 to 4.5
- readout: bfloat16 [4096, 8192], P('group', 'tensor'), may hold values from -0.0625 to 0.0625
- logit_base: float32 [4096], P('group'), may hold values from -3 to 3
- ref_logprob: float32 [4096], P('group'), may hold values from -3 to -0.1
- advantage: float32 [16], P('group'), may hold values from -3 to 3
- resp_length: int32 [16], P('group'), may hold values from 64 to 256, as said below
- token_count: int32 [1], replicated, may hold values from 2048 to 8191
Outputs:
- loss: float32 [1], replicated
- grad_query: bfloat16 [4096, 8192], P('group', 'tensor')
- grad_resp_key: bfloat16 [4096, 1024], P('group', 'tensor')
- grad_resp_value: bfloat16 [4096, 1024], P('group', 'tensor')
- grad_prefix_key: bfloat16 [4096, 1024], P('group', 'tensor')
- grad_prefix_value: bfloat16 [4096, 1024], P('group', 'tensor')
Inputs may be any that keep to these rules, and one draw needn't show every extreme that they name: `resp_length`: one response has exactly 256 tokens.
All inputs are finite; a program needn't handle non-finite values.
Results may differ from a plain program's by a relative error of at most 0.022.
Values may be sent and summed in bfloat16 or wider, within the bound.
A program may use at most 128 MiB of HBM per device.

v0:
```python
import jax
import jax.numpy as jnp
from jax import lax
from jax.sharding import PartitionSpec as P

DH = 128


score_floor = -1e30
grad_boost = 64.0


def judge(logit_value, ref_rows, is_valid, advantage_value, token_total, grad_factor):
    logprob = jax.nn.log_sigmoid(logit_value)
    log_gap = ref_rows - logprob
    token_terms = jnp.where(
        is_valid, jnp.exp(log_gap) - log_gap - 1.0 - advantage_value * logprob, 0.0
    )
    d_logit = jnp.where(
        is_valid, (1.0 - jnp.exp(log_gap) - advantage_value) * jax.nn.sigmoid(-logit_value), 0.0
    ) * (grad_factor / token_total)
    return (d_logit, token_terms)


def scores_of(queries, key_rows, score_scale, allowed):
    split_keys = key_rows.reshape(key_rows.shape[0], queries.shape[1], -1)
    scores = (
        jnp.einsum("rkgd,skd->kgrs", queries, split_keys, preferred_element_type=jnp.float32)
        * score_scale
    )
    if allowed is not None:
        scores = jnp.where(allowed, scores, score_floor)
    return scores


def absorb(softmax_state, queries, key_rows, value_rows, score_scale, allowed):
    running_max, running_sum, weighted = softmax_state
    scores = scores_of(queries, key_rows, score_scale, allowed)
    new_max = jnp.maximum(running_max, scores.max(-1, keepdims=True))
    exponent = jnp.exp(scores - new_max)
    rescale = jnp.exp(running_max - new_max)
    split_values = value_rows.reshape(value_rows.shape[0], queries.shape[1], -1)
    contrib = jnp.einsum(
        "kgrs,skd->kgrd",
        exponent.astype(jnp.bfloat16),
        split_values,
        preferred_element_type=jnp.float32,
    )
    return (
        new_max,
        running_sum * rescale + exponent.sum(-1, keepdims=True),
        weighted * rescale + contrib,
    )


def score_grads(queries, key_rows, value_rows, log_total, grad_out, row_dot, score_scale, allowed):
    scores = scores_of(queries, key_rows, score_scale, allowed)
    weights_full = jnp.exp(scores - log_total)
    split_values = value_rows.reshape(value_rows.shape[0], queries.shape[1], -1)
    d_probs = jnp.einsum(
        "kgrd,skd->kgrs", grad_out, split_values, preferred_element_type=jnp.float32
    )
    d_scores = (weights_full * (d_probs - row_dot)).astype(jnp.bfloat16)
    return (weights_full, d_scores)


def key_value_grads(queries, weights_full, d_scores, grad_out, score_scale, row_total):
    grad_values = jnp.einsum(
        "kgrs,kgrd->skd",
        weights_full.astype(jnp.bfloat16),
        grad_out,
        preferred_element_type=jnp.float32,
    )
    grad_keys = (
        jnp.einsum("kgrs,rkgd->skd", d_scores, queries, preferred_element_type=jnp.float32)
        * score_scale
    )
    return (grad_keys.reshape(row_total, -1), grad_values.reshape(row_total, -1))


def query_term(d_scores, key_rows, kv_heads):
    split_keys = key_rows.reshape(key_rows.shape[0], kv_heads, -1)
    return jnp.einsum("kgrs,skd->kgrd", d_scores, split_keys, preferred_element_type=jnp.float32)


def reverse_block(
    query_grad, queries, key_rows, value_rows, log_total, grad_out, row_dot, score_scale, allowed
):
    weights_full, d_scores = score_grads(
        queries, key_rows, value_rows, log_total, grad_out, row_dot, score_scale, allowed
    )
    query_grad = query_grad + query_term(d_scores, key_rows, queries.shape[1])
    grad_keys, grad_values = key_value_grads(
        queries, weights_full, d_scores, grad_out, score_scale, key_rows.shape[0]
    )
    return (query_grad, grad_keys, grad_values)


def on_device(
    query,
    resp_key,
    resp_value,
    prefix_key,
    prefix_value,
    readout,
    logit_base,
    ref_logprob,
    advantage,
    resp_length,
    token_count,
):
    tok_rows = query.shape[0]
    kv_width = resp_key.shape[1]
    kv_heads = kv_width // DH
    groups = query.shape[1] // kv_width
    score_scale = DH ** (-0.5)
    queries = query.reshape(tok_rows, kv_heads, groups, DH)
    members = lax.axis_size("group")
    grad_factor = grad_boost * (tok_rows * members)
    shard_rows = prefix_key.shape[0]
    merged = 1
    while members % (merged * 2) == 0 and merged * 2 * shard_rows <= 512:
        merged = merged * 2
    block_rows = shard_rows * merged
    block_count = members // merged
    causal = jnp.arange(tok_rows)[:, None] >= jnp.arange(tok_rows)[None, :]
    start_state = (
        jnp.full((kv_heads, groups, tok_rows, 1), score_floor, jnp.float32),
        jnp.zeros((kv_heads, groups, tok_rows, 1), jnp.float32),
        jnp.zeros((kv_heads, groups, tok_rows, DH), jnp.float32),
    )

    def forward_block(softmax_state, block_pair):
        return (
            absorb(softmax_state, queries, block_pair[0], block_pair[1], score_scale, None),
            None,
        )

    every_key, every_value = (
        lax.all_gather(prefix_key, "group", axis=0, tiled=True),
        lax.all_gather(prefix_value, "group", axis=0, tiled=True),
    )
    key_blocks = every_key.reshape(block_count, block_rows, kv_width)
    value_blocks = every_value.reshape(block_count, block_rows, kv_width)
    softmax_state, unused = lax.scan(forward_block, start_state, (key_blocks, value_blocks))
    softmax_state = absorb(softmax_state, queries, resp_key, resp_value, score_scale, causal)
    running_max, running_sum, weighted = softmax_state
    attended = weighted / running_sum
    weight_out = readout.reshape(tok_rows, kv_heads, groups, DH).astype(jnp.float32)
    partial_value = jnp.einsum("kgrd,rkgd->r", attended, weight_out)
    token_total = token_count[0].astype(jnp.float32)
    positions = jnp.arange(tok_rows)
    logit_value = lax.psum(partial_value, "tensor") + logit_base
    is_valid = positions < resp_length[0]
    d_logit, token_terms = judge(
        logit_value, ref_logprob, is_valid, advantage[0], token_total, grad_factor
    )
    loss_value = lax.psum(jnp.sum(token_terms), "group") / token_total
    grad_out = (d_logit[:, None] * readout.astype(jnp.float32)).astype(jnp.bfloat16)
    grad_out = grad_out.reshape(tok_rows, kv_heads, groups, DH).transpose(1, 2, 0, 3)
    row_dot = jnp.sum(grad_out.astype(jnp.float32) * attended, -1, keepdims=True)
    log_total = running_max + jnp.log(running_sum)
    key_blocks = every_key.reshape(block_count, block_rows, kv_width)
    value_blocks = every_value.reshape(block_count, block_rows, kv_width)
    query_grad = jnp.zeros((kv_heads, groups, tok_rows, DH), jnp.float32)

    def backward_block(query_grad, block_pair):
        query_grad, key_terms, value_terms = reverse_block(
            query_grad,
            queries,
            block_pair[0],
            block_pair[1],
            log_total,
            grad_out,
            row_dot,
            score_scale,
            None,
        )
        return (query_grad, (key_terms, value_terms))

    query_grad, block_terms = lax.scan(backward_block, query_grad, (key_blocks, value_blocks))
    prefix_total = block_count * block_rows
    key_terms = block_terms[0].reshape(prefix_total, kv_width)
    value_terms = block_terms[1].reshape(prefix_total, kv_width)
    summed_keys, summed_values = (
        lax.psum_scatter(
            key_terms.astype(jnp.bfloat16), "group", scatter_dimension=0, tiled=True
        ).astype(jnp.float32),
        lax.psum_scatter(
            value_terms.astype(jnp.bfloat16), "group", scatter_dimension=0, tiled=True
        ).astype(jnp.float32),
    )
    query_grad, own_keys, own_values = reverse_block(
        query_grad, queries, resp_key, resp_value, log_total, grad_out, row_dot, score_scale, causal
    )
    grad_query = (
        (query_grad * score_scale)
        .transpose(2, 0, 1, 3)
        .reshape(tok_rows, kv_heads * groups * DH)
        .astype(jnp.bfloat16)
    )
    return (
        loss_value.reshape(1),
        grad_query,
        own_keys.astype(jnp.bfloat16),
        own_values.astype(jnp.bfloat16),
        summed_keys.astype(jnp.bfloat16),
        summed_values.astype(jnp.bfloat16),
    )


def solution(mesh):
    in_specs = (
        P("group", "tensor"),
        P("group", "tensor"),
        P("group", "tensor"),
        P("group", "tensor"),
        P("group", "tensor"),
        P("group", "tensor"),
        P("group"),
        P("group"),
        P("group"),
        P("group"),
        P(),
    )
    out_specs = (
        P(),
        P("group", "tensor"),
        P("group", "tensor"),
        P("group", "tensor"),
        P("group", "tensor"),
        P("group", "tensor"),
    )
    return jax.shard_map(
        on_device, mesh=mesh, in_specs=in_specs, out_specs=out_specs, check_vma=False
    )
```

profile of v0, /device:TPU:0, one launch (start us, length us, event | category | flops | bytes accessed | tf_op | source)
XLA Modules:
  0.0 385.7 jit_solution(11863898227353061950)
XLA Ops:
  10.7 1.9 copy.72
  14.3 2.9 fusion.112
  17.1 38.4 %all-gather.3.cloned.1.call-done = bf16[4096,128]{1,0:T(8,128)(2,1)} async-done(((bf16[256,128]{1,0:T(8,128)(2,1)}), bf16[4096,128]{1,0:T(8,128)(2,1)}) %all-gather.3.cloned.1.call-update) | async-done | bytes 1048592 | tf_op jit(solution)/shard_map/all_gather | solution.py:140
  55.5 44.3 %all-gather.5.cloned.1.call-done = bf16[4096,128]{1,0:T(8,128)(2,1)} async-done(((bf16[256,128]{1,0:T(8,128)(2,1)}), bf16[4096,128]{1,0:T(8,128)(2,1)}) %all-gather.5.cloned.1.call-update) | async-done | bytes 1048592 | tf_op jit(solution)/shard_map/all_gather | solution.py:141
  99.8 36.3 %while.30 = (s32[]{:T(128)}, f32[1,8,256,1]{2,1,3,0:T(8,128)S(1)}, f32[1,8,256,1]{2,1,3,0:T(8,128)S(1)}, f32[1,8,256,128]{3,2,1,0:T(8,128)S(1)}, bf16[8,512,128]...) while((s32[]{:T(128)}, f32[1,8,256,1]{2,1,3,0:T(8,128)S(1)}, ...), condition=%wide.region_3.4_spmd.clone, body=%wide.region_0.3_spmd.clone.sunk | while | flops 546058240 | bytes 15597689 | solution.py:145
  99.8 1.6 bitcast_reduce_fusion.2
  102.2 2.1 fusion.143
  104.4 1.6 bitcast_reduce_fusion.2
  106.7 2.1 fusion.143
  108.9 1.6 bitcast_reduce_fusion.2
  111.2 2.1 fusion.143
  113.4 1.6 bitcast_reduce_fusion.2
  115.8 2.1 fusion.143
  118.0 1.6 bitcast_reduce_fusion.2
  120.3 2.1 fusion.143
  122.5 1.6 bitcast_reduce_fusion.2
  124.9 2.1 fusion.143
  127.1 1.6 bitcast_reduce_fusion.2
  129.4 2.1 fusion.143
  131.6 1.6 bitcast_reduce_fusion.2
  134.0 2.1 fusion.143
  137.5 2.0 fusion.76
  139.7 1.7 fusion.81
  142.8 2.4 multiply_reduce_fusion
  145.2 13.1 %psum.14 = f32[256]{0:T(256)S(1)} all-reduce(f32[256]{0:T(256)S(1)} %multiply_reduce_fusion), channel_id=1, replica_groups=mesh['group'=16,'tensor'=8] {'tensor'}, use_global_device_ids=true, to_apply=%region_6.7 | all-reduce | flops 256 | bytes 2048 | tf_op jit(solution)/shard_map/psum | solution.py:153
  163.0 68.3 %while.31 = (s32[]{:T(128)}, f32[1,8,256,128]{3,2,1,0:T(8,128)S(1)}, bf16[8,512,128]{2,1,0:T(8,128)(2,1)}, bf16[8,512,128]{2,1,0:T(8,128)(2,1)}, bf16[8,512,128]...) while((s32[]{:T(128)}, ...), condition=%wide.region_11.12_spmd.clone, body=%wide.region_10.11_spmd.clone.sunk | while | flops 1351155712 | bytes 24010908 | solution.py:181
  163.0 1.6 fusion.154
  166.0 2.0 fusion.155
  168.0 2.1 fusion.156
  171.5 1.6 fusion.154
  174.6 2.0 fusion.155
  176.6 2.1 fusion.156
  183.1 2.0 fusion.155
  185.1 2.1 fusion.156
  191.6 2.0 fusion.155
  193.6 2.1 fusion.156
  200.2 2.0 fusion.155
  202.1 2.1 fusion.156
  208.7 2.0 fusion.155
  210.7 2.1 fusion.156
  217.2 2.0 fusion.155
  219.2 2.1 fusion.156
  225.7 2.0 fusion.155
  227.7 2.1 fusion.156
  231.8 39.1 %psum.15 = f32[]{:T(128)} all-reduce(f32[]{:T(128)} %get-tuple-element.243), channel_id=1, replica_groups=mesh['group'=16,'tensor'=8] {'group'}, use_global_device_ids=true, to_apply=%region_8.9 | all-reduce | flops 1 | bytes 8 | tf_op jit(solution)/shard_map/psum | solution.py:158
  275.2 1.6 fusion.79
  279.3 22.3 %reduce-scatter.5.cloned.1.call-done = bf16[256,128]{1,0:T(8,128)(2,1)} async-done(((bf16[4096,128]{1,0:T(8,128)(2,1)}), bf16[256,128]{1,0:T(8,128)(2,1)}) %reduce-scatter.5.cloned.1.call-update) | async-done | bytes 65552 | tf_op jit(solution)/shard_map/reduce_scatter | solution.py:189
  301.6 76.4 %reduce-scatter.3.cloned.1.call-done = bf16[256,128]{1,0:T(8,128)(2,1)} async-done(((bf16[4096,128]{1,0:T(8,128)(2,1)}), bf16[256,128]{1,0:T(8,128)(2,1)}) %reduce-scatter.3.cloned.1.call-update) | async-done | bytes 65552 | tf_op jit(solution)/shard_map/reduce_scatter | solution.py:186
  (108 shorter events, 55.2 us)
Async XLA Ops:
  7.2 7.1 %copy-start = (bf16[256,128]{1,0:T(8,128)(2,1)S(1)}, bf16[256,128]{1,0:T(8,128)(2,1)}, u32[]{:S(2)}) copy-start(bf16[256,128]{1,0:T(8,128)(2,1)} %param.16) | copy-start | bytes 196612
  7.2 48.4 %all-gather.3.cloned.1.call-start = ((), (), s32[]{:S(2)}) async-start(), calls=%async_computation.2 | async-start | bytes 1114112 | tf_op jit(solution)/shard_map/all_gather | solution.py:140
  7.9 91.9 %all-gather.5.cloned.1.call-start = ((), (), s32[]{:S(2)}) async-start(), calls=%async_computation.3 | async-start | bytes 1114112 | tf_op jit(solution)/shard_map/all_gather | solution.py:141
  8.7 293.0 %reduce-scatter.5.cloned.1.call-start = ((), (), s32[]{:S(2)}) async-start(), calls=%async_computation.5 | async-start | bytes 1114112 | tf_op jit(solution)/shard_map/reduce_scatter | solution.py:189
  136.1 3.4 copy-start.8
  137.5 2.2 copy-start.1
  141.5 17.5 %copy-start.4 = (f32[1,8,256,128]{2,3,1,0:T(8,128)}, f32[1,8,256,128]{2,3,1,0:T(8,128)S(1)}, u32[]{:S(2)}) copy-start(f32[1,8,256,128]{2,3,1,0:T(8,128)S(1)} %fusion.81) | copy-start | bytes 3145732
  141.5 16.8 %copy-start.9 = (f32[256]{0:T(256)S(1)}, f32[256]{0:T(256)}, u32[]{:S(2)}) copy-start(f32[256]{0:T(256)} %param.22) | copy-start | bytes 3076
  141.5 16.8 %copy-start.10 = (f32[256]{0:T(256)S(1)}, f32[256]{0:T(256)}, u32[]{:S(2)}) copy-start(f32[256]{0:T(256)} %param.21) | copy-start | bytes 3076
  141.5 17.4 %copy-start.6 = (bf16[256,1024]{1,0:T(8,128)(2,1)S(1)}, bf16[256,1024]{1,0:T(8,128)(2,1)}, u32[]{:S(2)}) copy-start(bf16[256,1024]{1,0:T(8,128)(2,1)} %param.20) | copy-start | bytes 1572868
  161.1 1.8 copy-start.3
  231.2 40.4 %copy-start.2 = (f32[1,8,256,256]{2,3,1,0:T(8,128)S(1)}, f32[1,8,256,256]{2,3,1,0:T(8,128)}, u32[]{:S(2)}) copy-start(f32[1,8,256,256]{2,3,1,0:T(8,128)} %get-tuple-element.245) | copy-start | bytes 6291460
  231.2 146.8 %reduce-scatter.3.cloned.1.call-start = ((), (), s32[]{:S(2)}) async-start(), calls=%async_computation.4 | async-start | bytes 1114112 | tf_op jit(solution)/shard_map/reduce_scatter | solution.py:186
  275.2 1.6 copy-start.5
  276.9 1.4 copy-start.7
Sparse Core Ops, SparseCore 0:
  10.2 45.3 all-gather.2
  57.7 42.0 all-gather.4
  231.4 70.2 reduce-scatter.4
  305.6 72.3 reduce-scatter.2
where the time goes:
time: 387 us; the launch traced here: 386 us
  waiting for transfers between devices  183 us (47%)
  matrix products  107 us (28%)
  blocking collectives  52.2 us (13%)
  between operations  17.8 us (5%)
  other arithmetic  13.3 us (3%)
  local copies, waits for them, and re-layouts  10.9 us (3%)
    reduce_scatter x1, waiting for transfers between devices, on_device(): lax.psum_scatter(key_terms.astype(jnp.bfloat16), 'group', scatter_dimensi...  76.4 us
    all_gather x1, waiting for transfers between devices, on_device(): lax.all_gather(prefix_value, 'group', axis=0, tiled=True)  44.3 us
    psum x1, blocking collectives, on_device(): loss_value = lax.psum(jnp.sum(token_terms), 'group') / token_total  39.1 us
    all_gather x1, waiting for transfers between devices, on_device(): lax.all_gather(prefix_key, 'group', axis=0, tiled=True)  38.4 us
    dot_general x17, matrix products, scores_of(): jnp.einsum('rkgd,skd->kgrs', queries, split_keys, preferred_element_type=...  28.7 us
    reduce_scatter x1, waiting for transfers between devices, on_device(): lax.psum_scatter(value_terms.astype(jnp.bfloat16), 'group', scatter_dimen...  22.3 us
    dot_general x9, matrix products, absorb(): jnp.einsum('kgrs,skd->kgrd', exponent.astype(jnp.bfloat16), split_values,...  18.8 us
    dot_general x9, matrix products, score_grads(): jnp.einsum('kgrd,skd->kgrs', grad_out, split_values, preferred_element_ty...  17.6 us
  transfers between devices with their start and end apart: 4, of which 4 were waited for; matrix products, arithmetic and copies ran while one was open for 4% of the time, Pallas kernels for 0%

commit v1 on v0

v1 whole, which is shorter than its diff:
```python
import functools

import jax
import jax.numpy as jnp
from jax import lax
from jax.experimental import pallas as pl
from jax.experimental.pallas import tpu as pltpu
from jax.sharding import PartitionSpec as P

MESH = pl.DeviceIdType.MESH
bf16 = jnp.bfloat16
f32 = jnp.float32
NT = (((1,), (1,)), ((), ()))

DH = 128
TOK = 256
HPD = 8
ROWS = TOK * HPD
KEYS = 4096 + TOK
SIDE = 4
HALF = 128
STEPS = (1, 3, 2)
OWN_A, OWN_B, NEAR, FAR = 256, 384, 512, 1280
OWN, GROUP = 512, 768
LAST = 5
SCORE_SCALE = DH**-0.5
TO_LOG2 = SCORE_SCALE * 1.4426950408889634
SCORE_FLOOR = -1e30
GRAD_FACTOR = 64.0 * 4096.0


def block_at(b):
    if isinstance(b, int):
        return (0, OWN) if b == 0 else (OWN + GROUP * (b - 1), GROUP)
    return pl.multiple_of(OWN + GROUP * (b - 1), 256), GROUP


def fold_rows(x):
    return jnp.sum(x.reshape(-1, 8, x.shape[-1]), 0)


def cols(h, width):
    return slice(h * width, (h + 1) * width)


def score_stage(r, h, b, buf, first):
    row0, size = block_at(b)
    s = (
        lax.dot_general(
            r["kv"][pl.ds(row0, size), :DH],
            r["q"][:, cols(h, DH)],
            NT,
            preferred_element_type=f32,
        )
        * TO_LOG2
    )
    if first:
        key_at = lax.broadcasted_iota(jnp.int32, (TOK, TOK), 0)
        query_at = lax.broadcasted_iota(jnp.int32, (TOK, TOK), 1)
        s = jnp.concatenate([jnp.where(key_at <= query_at, s[:TOK], SCORE_FLOOR), s[TOK:]], 0)
    buf[:size, :] = s
    top = jnp.ceil(jnp.max(jnp.max(s.reshape(-1, 8, TOK), 0), 0, keepdims=True))
    if not first:
        top = jnp.maximum(top, r["top"][b - 1, h : h + 1, :])
    r["top"][b, h : h + 1, :] = top


def weight_stage(r, h, b, buf, first):
    row0, size = block_at(b)
    at = cols(h, TOK)
    along = lax.dot_general(
        r["kv"][pl.ds(row0, size), DH:],
        r["ro"][:, cols(h, DH)],
        NT,
        preferred_element_type=f32,
    )
    top = r["top"][b, h : h + 1, :]
    e = jnp.exp2(buf[:size, :] - top)
    r["e"][pl.ds(row0, size), at] = e.astype(bf16)
    r["along"][pl.ds(row0, size), at] = along
    if first:
        r["l"][:, at] = fold_rows(e)
        r["dot"][:, at] = fold_rows(e * along)
    else:
        shrink = jnp.exp2(r["top"][b - 1, h : h + 1, :] - top)
        r["l"][:, at] = r["l"][:, at] * shrink + fold_rows(e)
        r["dot"][:, at] = r["dot"][:, at] * shrink + fold_rows(e * along)


def forward_block(r, b, first=False):
    bufs = (r["s0"], r["s1"])
    score_stage(r, 0, b, bufs[0], first)
    for h in range(HPD):
        if h + 1 < HPD:
            score_stage(r, h + 1, b, bufs[(h + 1) % 2], first)
        weight_stage(r, h, b, bufs[h % 2], first)


def query_block(r, b, first=False):
    row0, size = block_at(b)
    rows = pl.ds(row0, size)
    r["kt"][:, :size] = jnp.transpose(r["kv"][rows, :DH].astype(f32)).astype(bf16)
    for h in range(HPD):
        at = cols(h, TOK)
        x = r["e"][rows, at].astype(f32) * (r["along"][rows, at] - r["mean"][h : h + 1, :])
        r["along"][rows, at] = x
        d = jnp.dot(r["kt"][:, :size], x.astype(bf16), preferred_element_type=f32)
        d = d * jnp.exp2(r["top"][b, h : h + 1, :] - r["top"][LAST, h : h + 1, :])
        r["dq"][:, at] = d if first else r["dq"][:, at] + d


def grads_block(r, b):
    row0, size = block_at(b)
    rows = pl.ds(row0, size)
    c = jnp.transpose(r["c"][...] * jnp.exp2(r["top"][b] - r["top"][LAST]))
    ck = c * SCORE_SCALE
    for h in range(HPD):
        at = cols(h, TOK)
        r["wv"][at, :] = (r["ro"][:, cols(h, DH)].astype(f32) * c[:, h : h + 1]).astype(bf16)
        r["wq"][at, :] = (r["q"][:, cols(h, DH)].astype(f32) * ck[:, h : h + 1]).astype(bf16)
    r["kv"][rows, DH:] = jnp.dot(
        r["e"][rows, :], r["wv"][...], preferred_element_type=f32
    ).astype(bf16)
    r["kv"][rows, :DH] = jnp.dot(
        r["along"][rows, :].astype(bf16), r["wq"][...], preferred_element_type=f32
    ).astype(bf16)


def judge(logit, ref_rows, is_valid, advantage, token_total):
    logprob = jnp.minimum(logit, 0.0) - jnp.log1p(jnp.exp(-jnp.abs(logit)))
    gap = ref_rows - logprob
    ratio = jnp.exp(gap)
    terms = jnp.where(is_valid, ratio - gap - 1.0 - advantage * logprob, 0.0)
    d_logit = jnp.where(
        is_valid, (1.0 - ratio - advantage) * jax.nn.sigmoid(-logit), 0.0
    ) * (GRAD_FACTOR / token_total)
    return d_logit, terms


NAMES = (
    ["e", "along", "kv", "q", "ro", "s0", "s1", "kt", "dq", "wv", "wq", "top", "l", "dot"]
    + ["mean", "c", "got", "got2", "part", "loss_z", "loss_y", "lb", "rf", "load_sem"]
    + ["ag_send", "ag_recv", "part_send", "part_recv", "rs_send", "rs_recv"]
    + ["rs2_send", "rs2_recv", "lz_send", "lz_recv", "ly_send", "ly_recv"]
)


def scratch():
    vm, dma = pltpu.VMEM, pltpu.SemaphoreType.DMA
    return [
        vm((KEYS, ROWS), bf16),
        vm((KEYS, ROWS), f32),
        vm((KEYS, 2 * DH), bf16),
        vm((TOK, HPD * DH), bf16),
        vm((TOK, HPD * DH), bf16),
        vm((GROUP, TOK), f32),
        vm((GROUP, TOK), f32),
        vm((DH, GROUP), bf16),
        vm((DH, ROWS), f32),
        vm((ROWS, DH), bf16),
        vm((ROWS, DH), bf16),
        vm((LAST + 1, HPD, TOK), f32),
        vm((8, ROWS), f32),
        vm((8, ROWS), f32),
        vm((HPD, TOK), f32),
        vm((HPD, TOK), f32),
        vm((4, GROUP, 2 * DH), bf16),
        vm((2, 3, HALF, 2 * DH), bf16),
        vm((8, 8, TOK), f32),
        vm((SIDE, 8, 128), f32),
        vm((SIDE, 8, 128), f32),
        vm((1, TOK), f32),
        vm((1, TOK), f32),
        dma((16,)),
        dma((30,)),
        dma((30,)),
        dma((8,)),
        dma((8,)),
        dma((24,)),
        dma((24,)),
        dma((6,)),
        dma((6,)),
        dma((3,)),
        dma((SIDE,)),
        dma((3,)),
        dma((SIDE,)),
    ]


def kernel(*refs):
    (q, ro, rk, rv, pk, pv, lb, rf, adv, rlen, count) = refs[:11]
    (loss, gq, grk, grv, gpk, gpv) = refs[11:17]
    r = dict(zip(NAMES, refs[17:]))
    kv = r["kv"]

    g, t = lax.axis_index("group"), lax.axis_index("tensor")
    y, z = g // SIDE, g % SIDE

    def along_z(step):
        return (y * SIDE + (z + step) % SIDE, t)

    def along_y(step):
        return (((y + step) % SIDE) * SIDE + z, t)

    def in_tensor(step):
        return (g, (t + step) % 8)

    moves = [
        (pk.at[:HALF], kv.at[OWN_A : OWN_A + HALF, :DH]),
        (pk.at[HALF:], kv.at[OWN_B : OWN_B + HALF, :DH]),
        (pv.at[:HALF], kv.at[OWN_A : OWN_A + HALF, DH:]),
        (pv.at[HALF:], kv.at[OWN_B : OWN_B + HALF, DH:]),
        (rk, kv.at[:TOK, :DH]),
        (rv, kv.at[:TOK, DH:]),
        (q, r["q"]),
        (ro, r["ro"]),
        (lb, r["lb"]),
        (rf, r["rf"]),
    ]
    loads = [
        pltpu.make_async_copy(src, dst, r["load_sem"].at[i]) for i, (src, dst) in enumerate(moves)
    ]
    for load in loads:
        load.start()

    barrier = pltpu.get_barrier_semaphore()
    peers = (
        [along_z(d) for d in STEPS]
        + [along_y(d) for d in STEPS]
        + [in_tensor(d) for d in range(1, 8)]
    )
    for peer in peers:
        pl.semaphore_signal(barrier, inc=1, device_id=peer, device_id_type=MESH)
    for load in loads[:4]:
        load.wait()
    pl.semaphore_wait(barrier, len(peers))

    def part_of_code(body):
        pl.when(t >= 0)(body)

    def remote(src, dst, send_sem, recv_sem, peer):
        return pltpu.make_async_remote_copy(
            src_ref=src,
            dst_ref=dst,
            send_sem=send_sem,
            recv_sem=recv_sem,
            device_id=peer,
            device_id_type=MESH,
        )

    def gather_copy(slot, src_row, dst_row, peer):
        return remote(
            kv.at[src_row : src_row + HALF],
            kv.at[dst_row : dst_row + HALF],
            r["ag_send"].at[slot],
            r["ag_recv"].at[slot],
            peer,
        )

    near = [gather_copy(j, OWN_A, NEAR + HALF * j, along_z(-STEPS[j])) for j in range(3)]
    near += [
        gather_copy(3 + j, OWN_B, NEAR + 384 + HALF * j, along_y(-STEPS[j])) for j in range(3)
    ]
    far = []
    for i in range(4):
        src_a = OWN_A if i == 0 else NEAR + HALF * (i - 1)
        src_b = OWN_B if i == 0 else NEAR + 384 + HALF * (i - 1)
        dst = FAR + GROUP * i
        far.append(
            [gather_copy(6 + 6 * i + k, src_a, dst + HALF * k, along_y(-STEPS[k])) for k in range(3)]
            + [
                gather_copy(9 + 6 * i + k, src_b, dst + 384 + HALF * k, along_z(-STEPS[k]))
                for k in range(3)
            ]
        )
    for copy in near + far[0]:
        copy.start()
    for load in loads[4:]:
        load.wait()

    part_of_code(lambda: forward_block(r, 0, True))

    def forward_step(b, carry):
        @pl.when(b == 1)
        def _():
            for j in range(3):
                near[j].wait_recv()
                near[3 + j].wait_recv()
                for copy in far[j + 1]:
                    copy.start()

        for i in range(4):

            @pl.when(b == 2 + i)
            def _():
                for copy in far[i]:
                    copy.wait_recv()

        forward_block(r, b)
        return carry

    lax.fori_loop(1, LAST + 1, forward_step, 0)

    total = jnp.zeros((1, TOK), f32)
    sums = []
    for h in range(HPD):
        at = cols(h, TOK)
        row_sum = jnp.sum(r["l"][:, at], 0, keepdims=True)
        mean = jnp.sum(r["dot"][:, at], 0, keepdims=True) / row_sum
        r["mean"][h : h + 1, :] = mean
        r["c"][h : h + 1, :] = 1.0 / row_sum
        total = total + mean
    part = r["part"]
    part[t] = jnp.broadcast_to(total, (8, TOK))
    part_copies = [
        remote(
            part.at[t], part.at[t], r["part_send"].at[d], r["part_recv"].at[d], in_tensor(d)
        )
        for d in range(1, 8)
    ]
    for copy in part_copies:
        copy.start()

    part_of_code(lambda: query_block(r, 0, True))

    def query_step(n, carry):
        query_block(r, (3 * n + 1) // 2 + 1)
        return carry

    lax.fori_loop(0, 3, query_step, 0)

    for copy in part_copies:
        copy.wait()
    logit = r["lb"][...]
    for i in range(8):
        logit = logit + part[i, 0:1, :]
    token_total = count[0].astype(f32)
    is_valid = lax.broadcasted_iota(jnp.int32, (1, TOK), 1) < rlen[0]
    d_logit, terms = judge(logit, r["rf"][...], is_valid, adv[0], token_total)
    r["c"][...] = r["c"][...] * d_logit

    loss_z, loss_y = r["loss_z"], r["loss_y"]
    loss_z[z] = jnp.broadcast_to(jnp.sum(terms, axis=1, keepdims=True), (8, 128))
    lz = [
        remote(
            loss_z.at[z], loss_z.at[z], r["lz_send"].at[j], r["lz_recv"].at[STEPS[j]], along_z(STEPS[j])
        )
        for j in range(3)
    ]
    for copy in lz:
        copy.start()

    for copy in near:
        copy.wait_send()
    for group in far:
        for copy in group:
            copy.wait_send()

    def spread(i):
        row0 = FAR + GROUP * i
        return [
            remote(
                kv.at[pl.ds(row0 + HALF * n, HALF)],
                r["got"].at[i, pl.ds(HALF * n, HALF)],
                r["rs_send"].at[6 * i + n],
                r["rs_recv"].at[6 * i + n],
                along_y(STEPS[n]) if n < 3 else along_z(STEPS[n - 3]),
            )
            for n in range(6)
        ]

    second = []

    def second_stage(i):
        for copy in spread(i):
            copy.wait_recv()
        for side in range(2):
            row0 = NEAR + 384 * side + HALF * (i - 1)
            acc = kv[row0 : row0 + HALF, :].astype(f32)
            for k in range(3):
                at = 384 * side + HALF * k
                acc = acc + r["got"][i, at : at + HALF, :].astype(f32)
            kv[row0 : row0 + HALF, :] = acc.astype(bf16)
            slot = 2 * (i - 1) + side
            copy = remote(
                kv.at[row0 : row0 + HALF],
                r["got2"].at[side, i - 1],
                r["rs2_send"].at[slot],
                r["rs2_recv"].at[slot],
                along_y(STEPS[i - 1]) if side else along_z(STEPS[i - 1]),
            )
            copy.start()
            second.append(copy)

    def early_step(i, carry):
        grads_block(r, 2 + i)
        for copy in spread(i):
            copy.start()
        return carry

    def late_step(n, carry):
        i = 3 - 3 * n
        query_block(r, 2 + i)
        grads_block(r, 2 + i)
        for copy in spread(i):
            copy.start()
        return carry

    lax.fori_loop(1, 3, early_step, 0)
    part_of_code(lambda: grads_block(r, 1))

    for copy in lz:
        copy.wait()
    loss_y[y] = loss_z[0] + loss_z[1] + loss_z[2] + loss_z[3]
    ly = [
        remote(
            loss_y.at[y], loss_y.at[y], r["ly_send"].at[j], r["ly_recv"].at[STEPS[j]], along_y(STEPS[j])
        )
        for j in range(3)
    ]
    for copy in ly:
        copy.start()

    lax.fori_loop(0, 2, late_step, 0)
    second_stage(1)
    second_stage(2)
    part_of_code(lambda: grads_block(r, 0))
    stores = [
        pltpu.make_async_copy(kv.at[:TOK, :DH], grk, r["load_sem"].at[0]),
        pltpu.make_async_copy(kv.at[:TOK, DH:], grv, r["load_sem"].at[1]),
    ]
    for store in stores:
        store.start()
    second_stage(3)

    for h in range(HPD):
        d = r["dq"][:, cols(h, TOK)] * (r["c"][h : h + 1, :] * SCORE_SCALE)
        r["q"][:, cols(h, DH)] = jnp.transpose(d).astype(bf16)
    store_q = pltpu.make_async_copy(r["q"], gq, r["load_sem"].at[2])
    store_q.start()

    for copy in ly:
        copy.wait()
    loss[...] = (loss_y[0] + loss_y[1] + loss_y[2] + loss_y[3])[:1, :1] / token_total

    for copy in spread(0):
        copy.wait_recv()
    for copy in second:
        copy.wait_recv()
    for side in range(2):
        row0 = OWN_B if side else OWN_A
        acc = kv[row0 : row0 + HALF, :].astype(f32)
        for k in range(3):
            at = 384 * side + HALF * k
            acc = acc + r["got"][0, at : at + HALF, :].astype(f32)
        for k in range(3):
            acc = acc + r["got2"][side, k].astype(f32)
        kv[row0 : row0 + HALF, :] = acc.astype(bf16)
        half = slice(HALF, 2 * HALF) if side else slice(0, HALF)
        for n, (out, lanes) in enumerate(((gpk, slice(0, DH)), (gpv, slice(DH, 2 * DH)))):
            store = pltpu.make_async_copy(
                kv.at[row0 : row0 + HALF, lanes], out.at[half], r["load_sem"].at[3 + 2 * side + n]
            )
            store.start()
            stores.append(store)

    for store in stores:
        store.wait()
    store_q.wait()
    for i in range(4):
        for copy in spread(i):
            copy.wait_send()
    for copy in second:
        copy.wait_send()


def hand_over(*refs):
    for src, dst in zip(refs[:5], refs[5:]):
        dst[...] = src[...]


def on_device(query, resp_key, resp_value, prefix_key, prefix_value, readout, base, ref, adv, rlen, count):
    hbm = pl.BlockSpec(memory_space=pl.ANY)
    smem = pl.BlockSpec(memory_space=pltpu.SMEM)
    like = lambda x: jax.ShapeDtypeStruct(x.shape, bf16)
    flops = 5 * 2 * KEYS * ROWS * DH
    loss, gq, grk, grv, gpk, gpv = pl.pallas_call(
        kernel,
        out_shape=(
            jax.ShapeDtypeStruct((1, 1), f32),
            like(query),
            like(resp_key),
            like(resp_value),
            like(prefix_key),
            like(prefix_value),
        ),
        in_specs=[hbm] * 8 + [smem] * 3,
        out_specs=(pl.BlockSpec(memory_space=pltpu.VMEM),) + (hbm,) * 5,
        scratch_shapes=scratch(),
        cost_estimate=pl.CostEstimate(
            flops=flops, bytes_accessed=4 * 2**20, transcendentals=KEYS * ROWS
        ),
        compiler_params=pltpu.CompilerParams(
            collective_id=0, has_side_effects=True, vmem_limit_bytes=64 * 2**20 - 2**17
        ),
    )(
        query,
        readout,
        resp_key,
        resp_value,
        prefix_key,
        prefix_value,
        base.reshape(1, TOK),
        ref.reshape(1, TOK),
        adv,
        rlen,
        count,
    )
    grads = pl.pallas_call(
        hand_over,
        out_shape=tuple(like(x) for x in (gq, grk, grv, gpk, gpv)),
        in_specs=[pl.BlockSpec(memory_space=pltpu.VMEM)] * 5,
        out_specs=(pl.BlockSpec(memory_space=pltpu.VMEM),) * 5,
    )(gq, grk, grv, gpk, gpv)
    return (loss.reshape(1),) + tuple(grads)


def solution(mesh):
    both = P("group", "tensor")
    one = P("group")
    in_specs = (both,) * 6 + (one,) * 4 + (P(),)
    out_specs = (P(),) + (both,) * 5
    return jax.shard_map(
        on_device, mesh=mesh, in_specs=in_specs, out_specs=out_specs, check_vma=False
    )
```

time: 387 us -> 60 us (0.16)
  waiting for transfers between devices: 183 us -> 0 us
  matrix products: 107 us -> 0 us
  Pallas kernels: 0 us -> 55.5 us
  blocking collectives: 52.2 us -> 0 us
  between operations: 17.8 us -> 4.35 us
  other arithmetic: 13.3 us -> 0 us
  local copies, waits for them, and re-layouts: 10.9 us -> 0 us
    dot_general x62 -> x0, matrix products: 107 us -> none  [the longest x17 28.7 us: scores_of(): jnp.einsum('rkgd,skd->kgrs', queries, split_keys, preferred_element_type=...]
    reduce_scatter x2 -> x0, waiting for transfers between devices: 98.7 us -> none  [the longest x1 76.4 us: on_device(): lax.psum_scatter(key_terms.astype(jnp.bfloat16), 'group', scatter_dimensi...]
    all_gather x2 -> x0, waiting for transfers between devices: 82.7 us -> none  [the longest x1 44.3 us: on_device(): lax.all_gather(prefix_value, 'group', axis=0, tiled=True)]
    pallas_call x0 -> x2, Pallas kernels: none -> 55.5 us  [the longest x1 53.5 us: on_device(): pl.pallas_call(kernel, out_shape=(jax.ShapeDtypeStruct((1, 1), f32), like...]
    psum x2 -> x0, blocking collectives: 52.2 us -> none  [the longest x1 39.1 us: on_device(): loss_value = lax.psum(jnp.sum(token_terms), 'group') / token_total]
    reduce_sum x10 -> x0, other arithmetic: 9.13 us -> none  [the longest x9 7.6 us: absorb(): exponent.sum(-1, keepdims=True)]
    unnamed x29 -> x0, local copies, waits for them, and re-layouts: 6.99 us -> none
  transfers between devices with their start and end apart: 4 -> 0, of which waited for: 4 -> 0; matrix products, arithmetic and copies ran while one was open for 4% -> 0% of each run, Pallas kernels for 0% -> 0%
where the time goes in v1:
time: 60 us; the launch traced here: 59.8 us
  Pallas kernels  55.5 us (92%)
  between operations  4.35 us (7%)
    pallas_call x1, Pallas kernels, on_device(): pl.pallas_call(kernel, out_shape=(jax.ShapeDtypeStruct((1, 1), f32), like...  53.5 us
    pallas_call x1, Pallas kernels, on_device(): pl.pallas_call(hand_over, out_shape=tuple((like(x) for x in (gq, grk, grv...  2 us

profile of v1, /device:TPU:0, one launch (start us, length us, event | category | flops | bytes accessed | tf_op | source)
XLA Modules:
  0.0 59.8 jit_solution(2920830039873796049)
XLA Ops:
  2.6 53.5 %shard_map.154 = (f32[1,1]{1,0:T(1,128)}, bf16[256,1024]{1,0:T(8,128)(2,1)}, bf16[256,128]{1,0:T(8,128)(2,1)}, bf16[256,128]{1,0:T(8,128)(2,1)}, bf16[256,128]{1,0:T(8,128)(2,1)}, /*index=5*/bf16[256,128]{1,0:T(8,128)(2,1)}) custom-call(bf16[256,1024]{1,0:T(8,128)(2,1)} %refs_0_.1, bf16[256,1024]{1,0:T(8,128)(2,1)} %refs_1_.1, bf16[256,128]{1,0:T(8,128)(2,1)} %refs_2_.1, ...), custom_call_target="tpu_custom_call" | custom-call | flops 11408506880 | bytes 4194304 | tf_op jit(solution)/shard_map/pallas_call | solution.py:487
  56.1 2.0 %shard_map.155 = (bf16[256,1024]{1,0:T(8,128)(2,1)}, bf16[256,128]{1,0:T(8,128)(2,1)}, bf16[256,128]{1,0:T(8,128)(2,1)}, bf16[256,128]{1,0:T(8,128)(2,1)}, bf16[256,128]{1,0:T(8,128)(2,1)}) custom-call(bf16[256,1024]{1,0:T(8,128)(2,1)} %get-tuple-element.18.refs_0_, bf16[256,128]{1,0:T(8,128)(2,1)} %get-tuple-element.19.refs_1_, ...), custom_call_target="tpu_custom_call" | custom-call | tf_op jit(solution)/shard_map/pallas_call | solution.py:519

commit v2 on v1

--- a/solution.py
+++ b/solution.py
@@ -22,7 +22,7 @@
 STEPS = (1, 3, 2)
 OWN_A, OWN_B, NEAR, FAR = 256, 384, 512, 1280
 OWN, GROUP = 512, 768
-LAST = 5
+LAST = 6
 SCORE_SCALE = DH**-0.5
 TO_LOG2 = SCORE_SCALE * 1.4426950408889634
 SCORE_FLOOR = -1e30
@@ -31,8 +31,13 @@
 
 def block_at(b):
     if isinstance(b, int):
-        return (0, OWN) if b == 0 else (OWN + GROUP * (b - 1), GROUP)
+        size = {0: OWN, 5: 512, 6: 256}.get(b, GROUP)
+        return (0 if b == 0 else FAR + GROUP * 3 + 512 if b == 6 else OWN + GROUP * (b - 1)), size
     return pl.multiple_of(OWN + GROUP * (b - 1), 256), GROUP
+
+
+def place(side, k):
+    return 512 + HALF * side if k == 2 else 256 * side + HALF * k
 
 
 def fold_rows(x):
@@ -109,15 +114,17 @@
         r["dq"][:, at] = d if first else r["dq"][:, at] + d
 
 
-def grads_block(r, b):
-    row0, size = block_at(b)
-    rows = pl.ds(row0, size)
+def factor_block(r, b):
     c = jnp.transpose(r["c"][...] * jnp.exp2(r["top"][b] - r["top"][LAST]))
     ck = c * SCORE_SCALE
     for h in range(HPD):
         at = cols(h, TOK)
         r["wv"][at, :] = (r["ro"][:, cols(h, DH)].astype(f32) * c[:, h : h + 1]).astype(bf16)
         r["wq"][at, :] = (r["q"][:, cols(h, DH)].astype(f32) * ck[:, h : h + 1]).astype(bf16)
+
+
+def grads(r, row0, size):
+    rows = slice(row0, row0 + size)
     r["kv"][rows, DH:] = jnp.dot(
         r["e"][rows, :], r["wv"][...], preferred_element_type=f32
     ).astype(bf16)
@@ -164,7 +171,7 @@
         vm((8, ROWS), f32),
         vm((HPD, TOK), f32),
         vm((HPD, TOK), f32),
-        vm((4, GROUP, 2 * DH), bf16),
+        vm((4, 2, 3, HALF, 2 * DH), bf16),
         vm((2, 3, HALF, 2 * DH), bf16),
         vm((8, 8, TOK), f32),
         vm((SIDE, 8, 128), f32),
@@ -220,9 +227,6 @@
     loads = [
         pltpu.make_async_copy(src, dst, r["load_sem"].at[i]) for i, (src, dst) in enumerate(moves)
     ]
-    for load in loads:
-        load.start()
-
     barrier = pltpu.get_barrier_semaphore()
     peers = (
         [along_z(d) for d in STEPS]
@@ -231,6 +235,8 @@
     )
     for peer in peers:
         pl.semaphore_signal(barrier, inc=1, device_id=peer, device_id_type=MESH)
+    for load in loads:
+        load.start()
     for load in loads[:4]:
         load.wait()
     pl.semaphore_wait(barrier, len(peers))
@@ -267,9 +273,12 @@
         src_b = OWN_B if i == 0 else NEAR + 384 + HALF * (i - 1)
         dst = FAR + GROUP * i
         far.append(
-            [gather_copy(6 + 6 * i + k, src_a, dst + HALF * k, along_y(-STEPS[k])) for k in range(3)]
+            [
+                gather_copy(6 + 6 * i + k, src_a, dst + place(0, k), along_y(-STEPS[k]))
+                for k in range(3)
+            ]
             + [
-                gather_copy(9 + 6 * i + k, src_b, dst + 384 + HALF * k, along_z(-STEPS[k]))
+                gather_copy(9 + 6 * i + k, src_b, dst + place(1, k), along_z(-STEPS[k]))
                 for k in range(3)
             ]
         )
@@ -289,7 +298,7 @@
                 for copy in far[j + 1]:
                     copy.start()
 
-        for i in range(4):
+        for i in range(3):
 
             @pl.when(b == 2 + i)
             def _():
@@ -299,7 +308,13 @@
         forward_block(r, b)
         return carry
 
-    lax.fori_loop(1, LAST + 1, forward_step, 0)
+    lax.fori_loop(1, 5, forward_step, 0)
+    for n in (0, 1, 3, 4):
+        far[3][n].wait_recv()
+    part_of_code(lambda: forward_block(r, 5))
+    for n in (2, 5):
+        far[3][n].wait_recv()
+    part_of_code(lambda: forward_block(r, 6))
 
     total = jnp.zeros((1, TOK), f32)
     sums = []
@@ -321,13 +336,8 @@
     for copy in part_copies:
         copy.start()
 
-    part_of_code(lambda: query_block(r, 0, True))
-
-    def query_step(n, carry):
-        query_block(r, (3 * n + 1) // 2 + 1)
-        return carry
-
-    lax.fori_loop(0, 3, query_step, 0)
+    for b in range(LAST + 1):
+        part_of_code(functools.partial(query_block, r, b, b == 0))
 
     for copy in part_copies:
         copy.wait()
@@ -356,17 +366,20 @@
         for copy in group:
             copy.wait_send()
 
-    def spread(i):
-        row0 = FAR + GROUP * i
+    def axis_of(side, step):
+        return along_z(step) if side else along_y(step)
+
+    def spread(i, numbers=range(3)):
         return [
             remote(
-                kv.at[pl.ds(row0 + HALF * n, HALF)],
-                r["got"].at[i, pl.ds(HALF * n, HALF)],
-                r["rs_send"].at[6 * i + n],
-                r["rs_recv"].at[6 * i + n],
-                along_y(STEPS[n]) if n < 3 else along_z(STEPS[n - 3]),
+                kv.at[pl.ds(FAR + GROUP * i + place(side, k), HALF)],
+                r["got"].at[i, side, k],
+                r["rs_send"].at[6 * i + 3 * side + k],
+                r["rs_recv"].at[6 * i + 3 * side + k],
+                axis_of(side, STEPS[k]),
             )
-            for n in range(6)
+            for side in range(2)
+            for k in numbers
         ]
 
     second = []
@@ -378,8 +391,7 @@
             row0 = NEAR + 384 * side + HALF * (i - 1)
             acc = kv[row0 : row0 + HALF, :].astype(f32)
             for k in range(3):
-                at = 384 * side + HALF * k
-                acc = acc + r["got"][i, at : at + HALF, :].astype(f32)
+                acc = acc + r["got"][i, side, k].astype(f32)
             kv[row0 : row0 + HALF, :] = acc.astype(bf16)
             slot = 2 * (i - 1) + side
             copy = remote(
@@ -387,27 +399,31 @@
                 r["got2"].at[side, i - 1],
                 r["rs2_send"].at[slot],
                 r["rs2_recv"].at[slot],
-                along_y(STEPS[i - 1]) if side else along_z(STEPS[i - 1]),
+                axis_of(1 - side, STEPS[i - 1]),
             )
             copy.start()
             second.append(copy)
 
-    def early_step(i, carry):
-        grads_block(r, 2 + i)
-        for copy in spread(i):
-            copy.start()
-        return carry
-
-    def late_step(n, carry):
-        i = 3 - 3 * n
-        query_block(r, 2 + i)
-        grads_block(r, 2 + i)
-        for copy in spread(i):
-            copy.start()
-        return carry
-
-    lax.fori_loop(1, 3, early_step, 0)
-    part_of_code(lambda: grads_block(r, 1))
+    def own_grads(b):
+        def body():
+            factor_block(r, b)
+            grads(r, *block_at(b))
+
+        part_of_code(body)
+
+    def first_piece():
+        factor_block(r, 3)
+        grads(r, FAR + GROUP, 512)
+
+    part_of_code(first_piece)
+    for copy in spread(1, range(2)):
+        copy.start()
+    part_of_code(lambda: grads(r, FAR + GROUP + 512, 256))
+    for copy in spread(1, range(2, 3)):
+        copy.start()
+    own_grads(4)
+    for copy in spread(2):
+        copy.start()
 
     for copy in lz:
         copy.wait()
@@ -421,23 +437,32 @@
     for copy in ly:
         copy.start()
 
-    lax.fori_loop(0, 2, late_step, 0)
+    own_grads(5)
+    for copy in spread(3, range(2)):
+        copy.start()
+    own_grads(6)
+    for copy in spread(3, range(2, 3)):
+        copy.start()
+    own_grads(2)
+    for copy in spread(0):
+        copy.start()
+    own_grads(1)
     second_stage(1)
-    second_stage(2)
-    part_of_code(lambda: grads_block(r, 0))
+    own_grads(0)
     stores = [
         pltpu.make_async_copy(kv.at[:TOK, :DH], grk, r["load_sem"].at[0]),
         pltpu.make_async_copy(kv.at[:TOK, DH:], grv, r["load_sem"].at[1]),
     ]
     for store in stores:
         store.start()
-    second_stage(3)
+    second_stage(2)
 
     for h in range(HPD):
         d = r["dq"][:, cols(h, TOK)] * (r["c"][h : h + 1, :] * SCORE_SCALE)
         r["q"][:, cols(h, DH)] = jnp.transpose(d).astype(bf16)
     store_q = pltpu.make_async_copy(r["q"], gq, r["load_sem"].at[2])
     store_q.start()
+    second_stage(3)
 
     for copy in ly:
         copy.wait()
@@ -451,8 +476,7 @@
         row0 = OWN_B if side else OWN_A
         acc = kv[row0 : row0 + HALF, :].astype(f32)
         for k in range(3):
-            at = 384 * side + HALF * k
-            acc = acc + r["got"][0, at : at + HALF, :].astype(f32)
+            acc = acc + r["got"][0, side, k].astype(f32)
         for k in range(3):
             acc = acc + r["got2"][side, k].astype(f32)
         kv[row0 : row0 + HALF, :] = acc.astype(bf16)
@@ -475,8 +499,24 @@
 
 
 def hand_over(*refs):
-    for src, dst in zip(refs[:5], refs[5:]):
-        dst[...] = src[...]
+    srcs, dsts, held, sems = refs[:5], refs[5:10], refs[10:15], refs[15]
+    pieces = [(0, slice(64 * n, 64 * n + 64)) for n in range(4)]
+    pieces += [(n, slice(0, TOK)) for n in range(1, 5)]
+    reads = [
+        pltpu.make_async_copy(srcs[n].at[rows], held[n].at[rows], sems.at[0, at])
+        for at, (n, rows) in enumerate(pieces)
+    ]
+    writes = [
+        pltpu.make_async_copy(held[n].at[rows], dsts[n].at[rows], sems.at[1, at])
+        for at, (n, rows) in enumerate(pieces)
+    ]
+    for read in reads:
+        read.start()
+    for read, write in zip(reads, writes):
+        read.wait()
+        write.start()
+    for write in writes:
+        write.wait()
 
 
 def on_device(query, resp_key, resp_value, prefix_key, prefix_value, readout, base, ref, adv, rlen, count):
@@ -519,8 +559,10 @@
     grads = pl.pallas_call(
         hand_over,
         out_shape=tuple(like(x) for x in (gq, grk, grv, gpk, gpv)),
-        in_specs=[pl.BlockSpec(memory_space=pltpu.VMEM)] * 5,
-        out_specs=(pl.BlockSpec(memory_space=pltpu.VMEM),) * 5,
+        in_specs=[hbm] * 5,
+        out_specs=(hbm,) * 5,
+        scratch_shapes=[pltpu.VMEM(x.shape, bf16) for x in (gq, grk, grv, gpk, gpv)]
+        + [pltpu.SemaphoreType.DMA((2, 8))],
     )(gq, grk, grv, gpk, gpv)
     return (loss.reshape(1),) + tuple(grads)
 

time: 60 us -> 59.8 us (level)
  no operation moved by 1% of the time
where the time goes in v2:
time: 59.8 us; the launch traced here: 59.6 us
  Pallas kernels  55.2 us (92%)
  between operations  4.35 us (7%)
    pallas_call x1, Pallas kernels, on_device(): pl.pallas_call(kernel, out_shape=(jax.ShapeDtypeStruct((1, 1), f32), like...  53.2 us
    pallas_call x1, Pallas kernels, on_device(): pl.pallas_call(hand_over, out_shape=tuple((like(x) for x in (gq, grk, grv...  1.97 us

profile of v2, /device:TPU:0, one launch (start us, length us, event | category | flops | bytes accessed | tf_op | source)
XLA Modules:
  0.0 59.6 jit_solution(33918711902129036)
XLA Ops:
  2.6 53.2 %shard_map.154 = (f32[1,1]{1,0:T(1,128)}, bf16[256,1024]{1,0:T(8,128)(2,1)}, bf16[256,128]{1,0:T(8,128)(2,1)}, bf16[256,128]{1,0:T(8,128)(2,1)}, bf16[256,128]{1,0:T(8,128)(2,1)}, /*index=5*/bf16[256,128]{1,0:T(8,128)(2,1)}) custom-call(bf16[256,1024]{1,0:T(8,128)(2,1)} %refs_0_.1, bf16[256,1024]{1,0:T(8,128)(2,1)} %refs_1_.1, bf16[256,128]{1,0:T(8,128)(2,1)} %refs_2_.1, ...), custom_call_target="tpu_custom_call" | custom-call | flops 11408506880 | bytes 4194304 | tf_op jit(solution)/shard_map/pallas_call | solution.py:527
  55.8 2.0 %shard_map.155 = (bf16[256,1024]{1,0:T(8,128)(2,1)}, bf16[256,128]{1,0:T(8,128)(2,1)}, bf16[256,128]{1,0:T(8,128)(2,1)}, bf16[256,128]{1,0:T(8,128)(2,1)}, bf16[256,128]{1,0:T(8,128)(2,1)}) custom-call(bf16[256,1024]{1,0:T(8,128)(2,1)} %get-tuple-element.18.refs_0_, bf16[256,128]{1,0:T(8,128)(2,1)} %get-tuple-element.19.refs_1_, ...), custom_call_target="tpu_custom_call" | custom-call | tf_op jit(solution)/shard_map/pallas_call | solution.py:559
